TPU v7x, 128 devices: a whole 4x4x4 slice. The times are simulated.
128 devices in a mesh: dp: 16 (over y, x), tensor: 8 (over z, core).
Axes of the slice: x: 4, y: 4, z: 4, core: 2. Of those that a mesh axis runs over, the one named last changes fastest.
Arguments:
- tokens: bfloat16 [8192, 2048], P('dp'), may hold values from -6 to 6
- segments: int32 [8192], P('dp'), may hold values from 0 to 8191, as said below
- weight_qkv: float32 [2048, 3072], P('dp', 'tensor'), may hold values from -0.125 to 0.125
- weight_out: float32 [2048, 2048], P('tensor', 'dp'), may hold values from -0.5 to 0.5
- weight_gate_up: float32 [2, 2048, 8192], P(None, 'dp', 'tensor'), may hold values from -0.125 to 0.125
- weight_down: float32 [8192, 2048], P('tensor', 'dp'), may hold values from -0.0625 to 0.0625
- norm_gains: float32 [2, 2048], replicated, may hold values from 0.5 to 1.5
- head_gains: float32 [2, 64], replicated, may hold values from 1 to 2
- first_qkv: float32 [2048, 3072], P('dp', 'tensor'), may hold values from -2048 to 2048
- first_out: float32 [2048, 2048], P('tensor', 'dp'), may hold values from -320 to 320
- first_gate_up: float32 [2, 2048, 8192], P(None, 'dp', 'tensor'), may hold values from -320 to 320
- first_down: float32 [8192, 2048], P('tensor', 'dp'), may hold values from -640 to 640
- first_norm: float32 [2, 2048], replicated, may hold values from -1536 to 1536
- first_head: float32 [2, 64], replicated, may hold values from -8192 to 8192
- second_qkv: float32 [2048, 3072], P('dp', 'tensor'), may hold values from 131072 to 524288
- second_out: float32 [2048, 2048], P('tensor', 'dp'), may hold values from 2949.12 to 11796.48
- second_gate_up: float32 [2, 2048, 8192], P(None, 'dp', 'tensor'), may hold values from 2949.12 to 11796.48
- second_down: float32 [8192, 2048], P('tensor', 'dp'), may hold values from 11796.48 to 47185.92
- second_norm: float32 [2, 2048], replicated, may hold values from 73728 to 294912
- second_head: float32 [2, 64], replicated, may hold values from 2097152 to 8388608
- cotangent: bfloat16 [8192, 2048], P('dp'), may hold values from -18 to 18
Outputs:
- block_out: bfloat16 [8192, 2048], P('dp')
- input_grad: bfloat16 [8192, 2048], P('dp')
- qkv_new: float32 [2048, 3072], P('dp', 'tensor')
- out_new: float32 [2048, 2048], P('tensor', 'dp')
- gate_up_new: float32 [2, 2048, 8192], P(None, 'dp', 'tensor')
- down_new: float32 [8192, 2048], P('tensor', 'dp')
- norm_gains_new: float32 [2, 2048], replicated
- head_gains_new: float32 [2, 64], replicated
- qkv_first: float32 [2048, 3072], P('dp', 'tensor')
- out_first: float32 [2048, 2048], P('tensor', 'dp')
- gate_up_first: float32 [2, 2048, 8192], P(None, 'dp', 'tensor')
- down_first: float32 [8192, 2048], P('tensor', 'dp')
- norm_first: float32 [2, 2048], replicated
- head_first: float32 [2, 64], replicated
- qkv_second: float32 [2048, 3072], P('dp', 'tensor')
- out_second: float32 [2048, 2048], P('tensor', 'dp')
- gate_up_second: float32 [2, 2048, 8192], P(None, 'dp', 'tensor')
- down_second: float32 [8192, 2048], P('tensor', 'dp')
- norm_second: float32 [2, 2048], replicated
- head_second: float32 [2, 64], replicated
- trust_stats: float32 [3, 6], replicated
Inputs may be any that keep to these rules, and one draw needn't show every extreme that they name: `segments`: segment numbers never fall and start at 0; the last document of the sequence has the number 8192 - 1; one document begins within the first 512 tokens and ends within the last 512 tokens, the others lie before or after it.
All inputs are finite; a program needn't handle non-finite values.
Results may differ from a plain program's by a relative error of at most 0.03.
Values may be sent and summed in bfloat16 or wider, within the bound.
No kernel may reach another device: no remote copies, remote signals or barrier semaphores. Data moves between devices by JAX's collectives and lax.ppermute only.
A program may use at most 576 MiB of HBM per device.

v0:
```python
import jax
import jax.numpy as jnp
from jax import lax
from jax.sharding import PartitionSpec as P

H = 32
KVH = 8
HD = 64
STEP = 5


EPS_NORM = 1e-05
ROPE_BASE = 1000000.0
BETA_ONE = 0.5
BETA_TWO = 0.5
EPS_ADAM = 1e-06
DECAY = 0.01
RATE = 0.5
MASKED = -1e30


def round_low(array_in):
    return lax.optimization_barrier(array_in.astype(jnp.bfloat16)).astype(jnp.float32)


def inverse_rms(array_in):
    return lax.rsqrt(jnp.mean(array_in * array_in, axis=-1, keepdims=True) + EPS_NORM)


def norm_back(grad_in, normed, inv_scale, gain):
    grad_hat = grad_in * gain
    return inv_scale * (grad_hat - normed * jnp.mean(grad_hat * normed, axis=-1, keepdims=True))


def rotary_tables(positions, width):
    half_width = width // 2
    frequency = ROPE_BASE ** (-(jnp.arange(half_width, dtype=jnp.float32) * 2.0 / width))
    angles = positions[:, None] * frequency[None, :]
    return (jnp.cos(angles), jnp.sin(angles))


def rotate(array_in, cosine, sine_table):
    half_width = array_in.shape[-1] // 2
    first_half = array_in[..., :half_width]
    second_half = array_in[..., half_width:]
    return jnp.concatenate(
        [
            first_half * cosine - second_half * sine_table,
            second_half * cosine + first_half * sine_table,
        ],
        axis=-1,
    )


def rotate_back(grad_in, cosine, sine_table):
    half_width = grad_in.shape[-1] // 2
    grad_first = grad_in[..., :half_width]
    grad_second = grad_in[..., half_width:]
    return jnp.concatenate(
        [
            grad_first * cosine + grad_second * sine_table,
            grad_second * cosine - grad_first * sine_table,
        ],
        axis=-1,
    )


def adapt(weight, first_old, second_old, grad_in):
    first_new = BETA_ONE * first_old + (1.0 - BETA_ONE) * grad_in
    second_new = BETA_TWO * second_old + (1.0 - BETA_TWO) * grad_in * grad_in
    direction = (
        first_new
        / (1.0 - BETA_ONE**STEP)
        / (jnp.sqrt(second_new / (1.0 - BETA_TWO**STEP)) + EPS_ADAM)
        + DECAY * weight
    )
    return (first_new, second_new, direction)


def local(
    tokens,
    segments,
    weight_qkv,
    weight_out,
    weight_gate_up,
    weight_down,
    norm_gains,
    head_gains,
    first_qkv,
    first_out,
    first_gate_up,
    first_down,
    first_norm,
    first_head,
    second_qkv,
    second_out,
    second_gate_up,
    second_down,
    second_norm,
    second_head,
    cotangent,
):
    local_rows = tokens.shape[0]
    seq_total = local_rows * lax.axis_size("dp")
    offset = lax.axis_index("dp") * local_rows
    per_group = H // KVH
    groups = weight_qkv.shape[1] // ((per_group + 2) * HD)
    query_count = per_group * local_rows
    score_scale = HD ** (-0.5)
    contract_rows = (((0,), (0,)), ((), ()))
    contract_cols = (((1,), (1,)), ((), ()))
    full_qkv, full_out, full_gate_up, full_down = (
        lax.all_gather(weight_qkv.astype(jnp.bfloat16), "dp", axis=0, tiled=True),
        lax.all_gather(weight_out.astype(jnp.bfloat16), "dp", axis=1, tiled=True),
        lax.all_gather(weight_gate_up.astype(jnp.bfloat16), "dp", axis=1, tiled=True),
        lax.all_gather(weight_down.astype(jnp.bfloat16), "dp", axis=1, tiled=True),
    )
    all_segments = lax.all_gather(segments, "dp", axis=0, tiled=True)
    inputs = tokens.astype(jnp.float32)
    scale_one = inverse_rms(inputs)
    normed_one = inputs * scale_one
    attn_in = (normed_one * norm_gains[0]).astype(jnp.bfloat16)
    projected = jnp.dot(attn_in, full_qkv, preferred_element_type=jnp.float32)
    projected = projected.reshape(local_rows, groups, per_group + 2, HD)
    queries = projected[:, :, :per_group]
    keys_raw = projected[:, :, per_group]
    values_raw = projected[:, :, per_group + 1]
    query_scale = inverse_rms(queries)
    query_hat = queries * query_scale
    key_scale = inverse_rms(keys_raw)
    key_hat = keys_raw * key_scale
    token_ids = offset + jnp.arange(local_rows, dtype=jnp.int32)
    cosine, sine_table = rotary_tables(token_ids.astype(jnp.float32), HD)
    cos_query = cosine[:, None, None, :]
    sin_query = sine_table[:, None, None, :]
    cos_key = cosine[:, None, :]
    sin_key = sine_table[:, None, :]
    query_rot = rotate(query_hat * head_gains[0], cos_query, sin_query)
    key_rot = rotate(key_hat * head_gains[1], cos_key, sin_key)
    query_rows = (
        query_rot.astype(jnp.bfloat16).transpose(1, 2, 0, 3).reshape(groups, query_count, HD)
    )
    local_kv = jnp.concatenate(
        [key_rot.astype(jnp.bfloat16), values_raw.astype(jnp.bfloat16)], axis=-1
    )
    all_kv = lax.all_gather(local_kv.transpose(1, 0, 2), "dp", axis=1, tiled=True)
    query_pos = jnp.tile(token_ids, per_group)
    query_seg = jnp.tile(segments, per_group)
    key_span = min(512, seq_total)
    block_count = (offset + local_rows - 1) // key_span + 1

    def block_scores(block_start):
        key_block = lax.dynamic_slice_in_dim(all_kv, block_start, key_span, 1)
        key_pos = block_start + jnp.arange(key_span, dtype=jnp.int32)
        key_seg = lax.dynamic_slice_in_dim(all_segments, block_start, key_span, 0)
        allowed = (key_pos[None, :] <= query_pos[:, None]) & (
            key_seg[None, :] == query_seg[:, None]
        )
        scores = (
            jnp.einsum(
                "gqd,gkd->gqk", query_rows, key_block[:, :, :HD], preferred_element_type=jnp.float32
            )
            * score_scale
        )
        return (key_block, allowed, jnp.where(allowed[None], scores, MASKED))

    def forward_step(block_index, carry):
        running_top, weight_sum, accum = carry
        key_block, allowed, scores = block_scores(block_index * key_span)
        new_top = jnp.maximum(running_top, jnp.max(scores, axis=-1))
        shrink_factor = jnp.exp(running_top - new_top)
        weights = jnp.where(allowed[None], jnp.exp(scores - new_top[..., None]), 0.0)
        weight_sum = weight_sum * shrink_factor + jnp.sum(weights, axis=-1)
        accum = accum * shrink_factor[..., None] + jnp.einsum(
            "gqk,gkd->gqd",
            weights.astype(jnp.bfloat16),
            key_block[:, :, HD:],
            preferred_element_type=jnp.float32,
        )
        return (new_top, weight_sum, accum)

    running_top, weight_sum, accum = lax.fori_loop(
        0,
        block_count,
        forward_step,
        (
            jnp.full((groups, query_count), MASKED, jnp.float32),
            jnp.zeros((groups, query_count), jnp.float32),
            jnp.zeros((groups, query_count, HD), jnp.float32),
        ),
    )
    log_total = running_top + jnp.log(weight_sum)
    attn_f = accum / weight_sum[..., None]
    mixed = attn_f.astype(jnp.bfloat16).reshape(groups, per_group, local_rows, HD)
    mixed = mixed.transpose(2, 0, 1, 3).reshape(local_rows, groups * per_group * HD)
    attn_total = lax.psum(
        jnp.dot(mixed, full_out, preferred_element_type=jnp.float32).astype(jnp.bfloat16), "tensor"
    ).astype(jnp.float32)
    hidden_one = inputs + attn_total
    scale_two = inverse_rms(hidden_one)
    normed_two = hidden_one * scale_two
    ffn_in = (normed_two * norm_gains[1]).astype(jnp.bfloat16)
    gate_value = jnp.dot(ffn_in, full_gate_up[0], preferred_element_type=jnp.float32)
    up_value = jnp.dot(ffn_in, full_gate_up[1], preferred_element_type=jnp.float32)
    sigmoid_gate = jax.nn.sigmoid(gate_value)
    activated = gate_value * sigmoid_gate
    inner_act = (activated * up_value).astype(jnp.bfloat16)
    ffn_total = lax.psum(
        jnp.dot(inner_act, full_down, preferred_element_type=jnp.float32).astype(jnp.bfloat16),
        "tensor",
    ).astype(jnp.float32)
    block_out = (hidden_one + ffn_total).astype(jnp.bfloat16)
    grad_inner = lax.dot_general(
        cotangent, full_down, contract_cols, preferred_element_type=jnp.float32
    )
    grad_down = lax.dot_general(
        inner_act, cotangent, contract_rows, preferred_element_type=jnp.float32
    )
    grad_gate = (
        grad_inner * up_value * sigmoid_gate * (1.0 + gate_value * (1.0 - sigmoid_gate))
    ).astype(jnp.bfloat16)
    grad_up = (grad_inner * activated).astype(jnp.bfloat16)
    grad_gate_up = jnp.stack(
        [
            lax.dot_general(ffn_in, grad_gate, contract_rows, preferred_element_type=jnp.float32),
            lax.dot_general(ffn_in, grad_up, contract_rows, preferred_element_type=jnp.float32),
        ]
    )
    ffn_part = lax.dot_general(
        grad_gate, full_gate_up[0], contract_cols, preferred_element_type=jnp.float32
    ) + lax.dot_general(grad_up, full_gate_up[1], contract_cols, preferred_element_type=jnp.float32)
    gain_ffn_part = jnp.sum(ffn_part * normed_two, axis=0)
    grad_ffn_in = lax.psum(ffn_part.astype(jnp.bfloat16), "tensor").astype(jnp.float32)
    grad_hidden = cotangent.astype(jnp.float32) + norm_back(
        grad_ffn_in, normed_two, scale_two, norm_gains[1]
    )
    grad_attn = grad_hidden.astype(jnp.bfloat16)
    grad_out_w = lax.dot_general(
        mixed, grad_attn, contract_rows, preferred_element_type=jnp.float32
    )
    grad_mixed = lax.dot_general(
        grad_attn, full_out, contract_cols, preferred_element_type=jnp.float32
    ).astype(jnp.bfloat16)
    grad_rows = (
        grad_mixed.reshape(local_rows, groups, per_group, HD)
        .transpose(1, 2, 0, 3)
        .reshape(groups, query_count, HD)
    )
    row_delta = jnp.sum(grad_rows.astype(jnp.float32) * attn_f, axis=-1)

    def backward_step(block_index, carry):
        grad_query, grad_kv = carry
        block_start = block_index * key_span
        key_block, allowed, scores = block_scores(block_start)
        attn_probs = jnp.where(allowed[None], jnp.exp(scores - log_total[..., None]), 0.0)
        grad_values = jnp.einsum(
            "gqk,gqd->gkd",
            attn_probs.astype(jnp.bfloat16),
            grad_rows,
            preferred_element_type=jnp.float32,
        )
        grad_probs = jnp.einsum(
            "gqd,gkd->gqk", grad_rows, key_block[:, :, HD:], preferred_element_type=jnp.float32
        )
        grad_scores = (attn_probs * (grad_probs - row_delta[..., None])).astype(jnp.bfloat16)
        grad_query = (
            grad_query
            + jnp.einsum(
                "gqk,gkd->gqd",
                grad_scores,
                key_block[:, :, :HD],
                preferred_element_type=jnp.float32,
            )
            * score_scale
        )
        grad_keys = (
            jnp.einsum("gqk,gqd->gkd", grad_scores, query_rows, preferred_element_type=jnp.float32)
            * score_scale
        )
        previous = lax.dynamic_slice_in_dim(grad_kv, block_start, key_span, 1)
        grad_kv = lax.dynamic_update_slice_in_dim(
            grad_kv, previous + jnp.concatenate([grad_keys, grad_values], axis=-1), block_start, 1
        )
        return (grad_query, grad_kv)

    grad_query, grad_kv = lax.fori_loop(
        0,
        block_count,
        backward_step,
        (
            jnp.zeros((groups, query_count, HD), jnp.float32),
            jnp.zeros((groups, seq_total, 2 * HD), jnp.float32),
        ),
    )
    grad_kv = round_low(
        lax.psum_scatter(
            grad_kv.astype(jnp.bfloat16), "dp", scatter_dimension=1, tiled=True
        ).astype(jnp.float32)
    )
    grad_key = grad_kv[:, :, :HD].transpose(1, 0, 2)
    grad_value = grad_kv[:, :, HD:].transpose(1, 0, 2)
    grad_query = (
        round_low(grad_query).reshape(groups, per_group, local_rows, HD).transpose(2, 0, 1, 3)
    )
    grad_qnorm = rotate_back(grad_query, cos_query, sin_query)
    gain_query = jnp.sum(grad_qnorm * query_hat, axis=(0, 1, 2))
    grad_queries = norm_back(grad_qnorm, query_hat, query_scale, head_gains[0])
    grad_knorm = rotate_back(grad_key, cos_key, sin_key)
    gain_key = jnp.sum(grad_knorm * key_hat, axis=(0, 1))
    grad_keys_raw = norm_back(grad_knorm, key_hat, key_scale, head_gains[1])
    grad_projected = jnp.concatenate(
        [grad_queries, grad_keys_raw[:, :, None], grad_value[:, :, None]], axis=2
    )
    grad_projected = grad_projected.reshape(local_rows, groups * (per_group + 2) * HD).astype(
        jnp.bfloat16
    )
    grad_qkv = lax.dot_general(
        attn_in, grad_projected, contract_rows, preferred_element_type=jnp.float32
    )
    attn_part = lax.dot_general(
        grad_projected, full_qkv, contract_cols, preferred_element_type=jnp.float32
    )
    gain_attn_part = jnp.sum(attn_part * normed_one, axis=0)
    grad_attn_in = lax.psum(attn_part.astype(jnp.bfloat16), "tensor").astype(jnp.float32)
    input_grad = (
        grad_hidden + norm_back(grad_attn_in, normed_one, scale_one, norm_gains[0])
    ).astype(jnp.bfloat16)
    grad_qkv, grad_out_w, grad_gate_up, grad_down = (
        lax.psum_scatter(
            grad_qkv.astype(jnp.bfloat16), "dp", scatter_dimension=0, tiled=True
        ).astype(jnp.float32),
        lax.psum_scatter(
            grad_out_w.astype(jnp.bfloat16), "dp", scatter_dimension=1, tiled=True
        ).astype(jnp.float32),
        lax.psum_scatter(
            grad_gate_up.astype(jnp.bfloat16), "dp", scatter_dimension=1, tiled=True
        ).astype(jnp.float32),
        lax.psum_scatter(
            grad_down.astype(jnp.bfloat16), "dp", scatter_dimension=1, tiled=True
        ).astype(jnp.float32),
    )
    matrices = (
        (weight_qkv, first_qkv, second_qkv, grad_qkv),
        (weight_out, first_out, second_out, grad_out_w),
        (weight_gate_up, first_gate_up, second_gate_up, grad_gate_up),
        (weight_down, first_down, second_down, grad_down),
    )
    adapted = [adapt(entry[0], entry[1], entry[2], entry[3]) for entry in matrices]
    squares = jnp.stack(
        [
            jnp.stack([jnp.sum(entry[0] * entry[0]) for entry in matrices]),
            jnp.stack([jnp.sum(item[2] * item[2]) for item in adapted]),
        ]
    )
    gain_norm_grad, gain_head_grad, square_sums = lax.psum(
        (jnp.stack([gain_attn_part, gain_ffn_part]), jnp.stack([gain_query, gain_key]), squares),
        ("dp", "tensor"),
    )
    weight_norms = [jnp.sqrt(square_sums[0, index]) for index in range(4)]
    step_norms = [jnp.sqrt(square_sums[1, index]) for index in range(4)]
    gain_sets = (
        (norm_gains, first_norm, second_norm, gain_norm_grad),
        (head_gains, first_head, second_head, gain_head_grad),
    )
    for entry in gain_sets:
        first_new, second_new, direction = adapt(entry[0], entry[1], entry[2], entry[3])
        adapted.append((first_new, second_new, direction))
        weight_norms.append(jnp.sqrt(jnp.sum(entry[0] * entry[0])))
        step_norms.append(jnp.sqrt(jnp.sum(direction * direction)))
    params = (weight_qkv, weight_out, weight_gate_up, weight_down, norm_gains, head_gains)
    ratios = [weight_norms[index] / (step_norms[index] + EPS_ADAM) for index in range(6)]
    new_params = [params[index] - RATE * ratios[index] * adapted[index][2] for index in range(6)]
    trust_stats = jnp.stack([jnp.stack(weight_norms), jnp.stack(step_norms), jnp.stack(ratios)])
    return (
        block_out,
        input_grad,
        new_params[0],
        new_params[1],
        new_params[2],
        new_params[3],
        new_params[4],
        new_params[5],
        adapted[0][0],
        adapted[1][0],
        adapted[2][0],
        adapted[3][0],
        adapted[4][0],
        adapted[5][0],
        adapted[0][1],
        adapted[1][1],
        adapted[2][1],
        adapted[3][1],
        adapted[4][1],
        adapted[5][1],
        trust_stats,
    )


def solution(mesh):
    in_specs = (
        P("dp", None),
        P("dp"),
        P("dp", "tensor"),
        P("tensor", "dp"),
        P(None, "dp", "tensor"),
        P("tensor", "dp"),
        P(),
        P(),
        P("dp", "tensor"),
        P("tensor", "dp"),
        P(None, "dp", "tensor"),
        P("tensor", "dp"),
        P(),
        P(),
        P("dp", "tensor"),
        P("tensor", "dp"),
        P(None, "dp", "tensor"),
        P("tensor", "dp"),
        P(),
        P(),
        P("dp", None),
    )
    out_specs = (
        P("dp", None),
        P("dp", None),
        P("dp", "tensor"),
        P("tensor", "dp"),
        P(None, "dp", "tensor"),
        P("tensor", "dp"),
        P(),
        P(),
        P("dp", "tensor"),
        P("tensor", "dp"),
        P(None, "dp", "tensor"),
        P("tensor", "dp"),
        P(),
        P(),
        P("dp", "tensor"),
        P("tensor", "dp"),
        P(None, "dp", "tensor"),
        P("tensor", "dp"),
        P(),
        P(),
        P(),
    )
    return jax.shard_map(local, mesh=mesh, in_specs=in_specs, out_specs=out_specs, check_vma=False)
```

profile of v0, /device:TPU:1, one launch (start us, length us, event | category | flops | bytes accessed | tf_op | source)
XLA Modules:
  0.0 1527.9 jit_solution(7623667715758735230)
XLA Ops:
  12.7 44.2 %all-gather.8.cloned.1.call-done = bf16[2048,384]{1,0:T(8,128)(2,1)} async-done(((bf16[128,384]{1,0:T(8,128)(2,1)}), bf16[2048,384]{1,0:T(8,128)(2,1)}) %all-gather.8.cloned.1.call-update) | async-done | bytes 1572880 | tf_op jit(solution)/shard_map/all_gather | solution.py:113
  62.4 17.5 %all-gather.1 = s32[16,1,512]{2,1,0:T(1,128)S(1)} all-gather(s32[1,1,512]{2,1,0:T(1,128)S(1)} %bitcast.334), channel_id=1, replica_groups=mesh['dp'=16,'tensor'=8] {'dp'}, dimensions={0}, use_global_device_ids=true | all-gather | bytes 34816 | tf_op jit(solution)/shard_map/all_gather | solution.py:118
  80.9 27.5 %all-gather.16.cloned.1.call-done = bf16[8192,1,128]{0,2,1:T(8,128)(2,1)} async-done(((bf16[512,1,128]{0,2,1:T(8,128)(2,1)}), bf16[8192,1,128]{0,2,1:T(8,128)(2,1)}) %all-gather.16.cloned.1.call-update) | async-done | bytes 2097168 | tf_op jit(solution)/shard_map/all_gather | solution.py:146
  118.6 34.6 %all-gather.10.cloned.1.call-done = bf16[256,2048]{1,0:T(8,128)(2,1)} async-done(((bf16[256,128]{1,0:T(8,128)(2,1)}), bf16[256,2048]{1,0:T(8,128)(2,1)}) %all-gather.10.cloned.1.call-update) | async-done | bytes 1048592 | tf_op jit(solution)/shard_map/all_gather | solution.py:114
  160.0 96.7 %all-reduce.6.cloned.1.call-done = bf16[512,2048]{1,0:T(8,128)(2,1)} async-done(((bf16[512,2048]{1,0:T(8,128)(2,1)}), bf16[512,2048]{1,0:T(8,128)(2,1)}) %all-reduce.6.cloned.1.call-update) | async-done | bytes 2097168 | tf_op jit(solution)/shard_map/psum | solution.py:196
  261.6 69.7 %all-gather.12.cloned.1.call-done = bf16[2,2048,1024]{2,1,0:T(8,128)(2,1)} async-done(((bf16[2,128,1024]{2,1,0:T(8,128)(2,1)}), bf16[2,2048,1024]{2,1,0:T(8,128)(2,1)}) %all-gather.12.cloned.1.call-update) | async-done | bytes 8388624 | tf_op jit(solution)/shard_map/all_gather | solution.py:115
  331.3 6.6 fusion.56
  341.6 48.5 %all-gather.14.cloned.1.call-done = bf16[1024,2048]{1,0:T(8,128)(2,1)} async-done(((bf16[1024,128]{1,0:T(8,128)(2,1)}), bf16[1024,2048]{1,0:T(8,128)(2,1)}) %all-gather.14.cloned.1.call-update) | async-done | bytes 4194320 | tf_op jit(solution)/shard_map/all_gather | solution.py:116
  390.1 8.1 multiply_convert_fusion.1
  403.5 7.3 fusion.104
  411.3 64.0 %all-reduce.8.cloned.1.call-done = bf16[512,2048]{1,0:T(8,128)(2,1)} async-done(((bf16[512,2048]{1,0:T(8,128)(2,1)}), bf16[512,2048]{1,0:T(8,128)(2,1)}) %all-reduce.8.cloned.1.call-update) | async-done | bytes 2097168 | tf_op jit(solution)/shard_map/psum | solution.py:233
  493.0 9.3 while.29
  502.4 11.6 convert_element_type.193
  514.0 206.8 %copy.97 = bf16[1,8192,128]{0,2,1:T(8,128)(2,1)} copy(bf16[1,8192,128]{1,0,2:T(2,128)(2,1)} %convert_element_type.193) | data formatting | bytes 4194304
  720.8 87.0 %bitcast_reduce_fusion = bf16[8192,128]{1,0:T(8,128)(2,1)} fusion(bf16[1,8192,128]{0,2,1:T(8,128)(2,1)} %copy.97), kind=kLoop, calls=%fused_computation.57 | loop fusion | bytes 4194304
  816.9 202.2 %reduce-scatter.16.cloned.1.call-done = bf16[512,128]{1,0:T(8,128)(2,1)} async-done(((bf16[8192,128]{1,0:T(8,128)(2,1)}), bf16[512,128]{1,0:T(8,128)(2,1)}) %reduce-scatter.16.cloned.1.call-update) | async-done | bytes 131088
  1019.1 13.2 reshape_bitcast_fusion
  1032.3 17.4 %copy.98 = bf16[1,512,128]{1,0,2:T(2,128)(2,1)S(1)} copy(bf16[1,512,128]{0,2,1:T(8,128)(2,1)} %reshape_bitcast_fusion) | data formatting | bytes 262144
  1083.6 7.5 pad_maximum_fusion
  1097.8 72.2 %all-reduce.10.cloned.1.call-done = (bf16[512,2048]{1,0:T(8,128)(2,1)}, bf16[512,2048]{1,0:T(8,128)(2,1)}) async-done(((bf16[512,2048]{1,0:T(8,128)(2,1)}, bf16[512,2048]{1,0:T(8,128)(2,1)}), (bf16[512,2048]{1,0:T(8,128)(2,1)}, bf16[512,2048]{1,0:T(8,128)(2,1)})) %all-reduce.10.cloned.1.call-update) | async-done | bytes 4194320 | tf_op jit(solution)/shard_map/psum | solution.py:208
  1174.7 76.2 %reduce-scatter.20.cloned.1.call-done = bf16[128,1024]{1,0:T(8,128)(2,1)} async-done(((bf16[2048,1024]{1,0:T(8,128)(2,1)}), bf16[128,1024]{1,0:T(8,128)(2,1)}) %reduce-scatter.20.cloned.1.call-update) | async-done | bytes 262160
  1252.7 74.5 %reduce-scatter.12.cloned.1.call-done = bf16[128,384]{1,0:T(8,128)(2,1)} async-done(((bf16[2048,384]{1,0:T(8,128)(2,1)}), bf16[128,384]{1,0:T(8,128)(2,1)}) %reduce-scatter.12.cloned.1.call-update) | async-done | bytes 98320 | tf_op jit(solution)/shard_map/reduce_scatter | solution.py:329
  1333.1 82.3 %reduce-scatter.14.cloned.1.call-done = bf16[2,128,1024]{2,1,0:T(8,128)(2,1)} async-done(((bf16[2,2048,1024]{2,1,0:T(8,128)(2,1)}), bf16[2,128,1024]{2,1,0:T(8,128)(2,1)}) %reduce-scatter.14.cloned.1.call-update) | async-done | bytes 524304 | tf_op jit(solution)/shard_map/reduce_scatter | solution.py:335
  1431.7 66.5 %all-reduce = (f32[2,4]{1,0:T(2,128)S(1)}, f32[2,2048]{1,0:T(2,128)}, f32[2,64]{1,0:T(2,128)S(1)}) all-reduce(f32[2,4]{1,0:T(2,128)} %pad_maximum_fusion.7, f32[2,2048]{1,0:T(2,128)S(1)} %pad_maximum_fusion.5, f32[2,64]{1,0:T(2,128)} %pad_maximum_fusion.8), channel_id=1, replica_groups=mesh['dp'=16,'tensor'=8] {'dp','tensor'}, use_global_device_ids=true, to_apply=%region_32.33 | all-reduce | flops 4232 | bytes 33856 | tf_op jit(solution)/shard_map/psum | solution.py:355
  (275 shorter events, 166.4 us)
Async XLA Ops:
  7.2 49.7 %all-gather.8.cloned.1.call-start = ((), (), s32[]{:S(2)}) async-start(), calls=%async_computation.5 | async-start | bytes 1671168 | tf_op jit(solution)/shard_map/all_gather | solution.py:113
  8.8 99.6 %all-gather.16.cloned.1.call-start = ((), (), s32[]{:S(2)}) async-start(), calls=%async_computation.13 | async-start | bytes 2228224 | tf_op jit(solution)/shard_map/all_gather | solution.py:146
  9.7 70.3 %copy-start.51 = (f32[64]{0:T(128)}, f32[64]{0:T(128)S(1)}, u32[]{:S(2)}) copy-start(f32[64]{0:T(128)S(1)} %get-tuple-element.429) | copy-start | bytes 772
  61.3 92.0 %all-gather.10.cloned.1.call-start = ((), (), s32[]{:S(2)}) async-start(), calls=%async_computation.6 | async-start | bytes 1114112 | tf_op jit(solution)/shard_map/all_gather | solution.py:114
  62.0 194.7 %all-reduce.6.cloned.1.call-start = ((), (), s32[]{:S(2)}) async-start(), calls=%async_computation.7 | async-start | bytes 4194304 | tf_op jit(solution)/shard_map/psum | solution.py:196
  153.3 103.4 %copy-start = (bf16[512,2048]{1,0:T(8,128)(2,1)S(1)}, bf16[512,2048]{1,0:T(8,128)(2,1)}, u32[]{:S(2)}) copy-start(bf16[512,2048]{1,0:T(8,128)(2,1)} %param.25) | copy-start | bytes 6291460
  156.7 174.5 %all-gather.12.cloned.1.call-start = ((), (), s32[]{:S(2)}) async-start(), calls=%async_computation.8 | async-start | bytes 8912896 | tf_op jit(solution)/shard_map/all_gather | solution.py:115
  158.9 231.2 %all-gather.14.cloned.1.call-start = ((), (), s32[]{:S(2)}) async-start(), calls=%async_computation.9 | async-start | bytes 4456448 | tf_op jit(solution)/shard_map/all_gather | solution.py:116
  159.7 315.6 %all-reduce.8.cloned.1.call-start = ((), (), s32[]{:S(2)}) async-start(), calls=%async_computation.10 | async-start | bytes 4194304 | tf_op jit(solution)/shard_map/psum | solution.py:233
  410.9 608.2 %reduce-scatter.16.cloned.1.call-start = ((), (), s32[]{:S(2)}) async-start(), calls=%async_computation.14 | async-start | bytes 2228224
  720.8 87.0 %copy-start.61 = (bf16[512,1024]{1,0:T(8,128)(2,1)S(1)}, bf16[512,1024]{1,0:T(8,128)(2,1)}, u32[]{:S(2)}) copy-start(bf16[512,1024]{1,0:T(8,128)(2,1)} %get-tuple-element.402) | copy-start | bytes 3145732
  807.8 287.0 %reduce-scatter.18.cloned.1.call-start = ((), (), s32[]{:S(2)}) async-start(), calls=%async_computation.15 | async-start | bytes 1114112
  816.6 353.3 %all-reduce.10.cloned.1.call-start = ((), (), s32[]{:S(2)}) async-start(), calls=%async_computation.17 | async-start | bytes 8388608 | tf_op jit(solution)/shard_map/psum | solution.py:208
  1056.3 194.5 %reduce-scatter.20.cloned.1.call-start = ((), (), s32[]{:S(2)}) async-start(), calls=%async_computation.16 | async-start | bytes 4456448
  1068.4 258.8 %reduce-scatter.12.cloned.1.call-start = ((), (), s32[]{:S(2)}) async-start(), calls=%async_computation.11 | async-start | bytes 1671168 | tf_op jit(solution)/shard_map/reduce_scatter | solution.py:329
  1072.6 342.8 %reduce-scatter.14.cloned.1.call-start = ((), (), s32[]{:S(2)}) async-start(), calls=%async_computation.12 | async-start | bytes 8912896 | tf_op jit(solution)/shard_map/reduce_scatter | solution.py:335
  1170.0 157.2 %copy-start.26 = (f32[128,384]{1,0:T(8,128)S(1)}, f32[128,384]{1,0:T(8,128)}, u32[]{:S(2)}) copy-start(f32[128,384]{1,0:T(8,128)} %param.27) | copy-start | bytes 589828
  1174.1 241.3 %copy-start.9 = (f32[2,128,1024]{2,1,0:T(8,128)S(1)}, f32[2,128,1024]{2,1,0:T(8,128)}, u32[]{:S(2)}) copy-start(f32[2,128,1024]{2,1,0:T(8,128)} %param.29) | copy-start | bytes 3145732
  1425.8 78.7 %copy-start.50 = (f32[2,64]{1,0:T(2,128)S(1)}, f32[2,64]{1,0:T(2,128)}, u32[]{:S(2)}) copy-start(f32[2,64]{1,0:T(2,128)} %param.32) | copy-start | bytes 1540
  1425.8 82.0 %copy-start.34 = (f32[2,2048]{1,0:T(2,128)S(1)}, f32[2,2048]{1,0:T(2,128)}, u32[]{:S(2)}) copy-start(f32[2,2048]{1,0:T(2,128)} %param.31) | copy-start | bytes 49156
  1425.8 82.0 %copy-start.48 = (f32[2,2048]{1,0:T(2,128)S(1)}, f32[2,2048]{1,0:T(2,128)}, u32[]{:S(2)}) copy-start(f32[2,2048]{1,0:T(2,128)} %param.37) | copy-start | bytes 49156
  1425.8 82.0 %copy-start.49 = (f32[2,2048]{1,0:T(2,128)S(1)}, f32[2,2048]{1,0:T(2,128)}, u32[]{:S(2)}) copy-start(f32[2,2048]{1,0:T(2,128)} %param.43) | copy-start | bytes 49156
  1431.7 87.6 %copy-start.17 = (f32[2,128,1024]{2,1,0:T(8,128)S(1)}, f32[2,128,1024]{2,1,0:T(8,128)}, u32[]{:S(2)}) copy-start(f32[2,128,1024]{2,1,0:T(8,128)} %get-tuple-element.390) | copy-start | bytes 3145732
  1431.7 87.6 %copy-start.18 = (f32[2,128,1024]{2,1,0:T(8,128)S(1)}, f32[2,128,1024]{2,1,0:T(8,128)}, u32[]{:S(2)}) copy-start(f32[2,128,1024]{2,1,0:T(8,128)} %get-tuple-element.391) | copy-start | bytes 3145732
  (51 other events, 741.3 us)
Sparse Core Ops, SparseCore 0:
  10.7 46.0 all-gather.7
  61.4 46.9 all-gather.15
  111.1 42.1 all-gather.9
  156.8 99.8 all-reduce.5
  259.3 71.9 all-gather.11
  333.8 56.2 all-gather.13
  411.0 64.3 all-reduce.7
  807.9 211.1 reduce-scatter.15
  1022.6 72.1 reduce-scatter.17
  1097.6 72.2 all-reduce.9
  1173.3 77.5 reduce-scatter.19
  1254.3 72.8 reduce-scatter.11
  1330.9 84.4 reduce-scatter.13
where the time goes:
time: 1540 us; the launch traced here: 1530 us
  waiting for transfers between devices  896 us (58%)
  local copies, waits for them, and re-layouts  356 us (23%)
  other arithmetic  86.2 us (6%)
  blocking collectives  84 us (5%)
  matrix products  79.1 us (5%)
  between operations  23.9 us (2%)
    unnamed x136, local copies, waits for them, and re-layouts  343 us
    unnamed x16, waiting for transfers between devices  282 us
    psum x1, waiting for transfers between devices, local(): lax.psum(jnp.dot(mixed, full_out, preferred_element_type=jnp.float32).ast...  96.7 us
    reduce_scatter x1, waiting for transfers between devices, local(): lax.psum_scatter(grad_gate_up.astype(jnp.bfloat16), 'dp', scatter_dimensi...  82.3 us
    reduce_scatter x1, waiting for transfers between devices, local(): lax.psum_scatter(grad_qkv.astype(jnp.bfloat16), 'dp', scatter_dimension=0...  74.5 us
    psum x1, waiting for transfers between devices, local(): lax.psum(jnp.dot(inner_act, full_down, preferred_element_type=jnp.float32...  72.2 us
    all_gather x1, waiting for transfers between devices, local(): lax.all_gather(weight_gate_up.astype(jnp.bfloat16), 'dp', axis=1, tiled=T...  69.7 us
    psum x1, blocking collectives, local(): lax.psum((jnp.stack([gain_attn_part, gain_ffn_part]), jnp.stack([gain_que...  66.5 us
  transfers between devices with their start and end apart: 13, of which 13 were waited for; matrix products, arithmetic and copies ran while one was open for 8% of the time, Pallas kernels for 0%

commit v1 on v0

v1 whole, which is shorter than its diff:
```python
import functools

import jax
import jax.numpy as jnp
from jax import lax
from jax.experimental import pallas as pl
from jax.experimental.pallas import tpu as pltpu
from jax.sharding import PartitionSpec as P

H = 32
KVH = 8
HD = 64
STEP = 5
D = 2048
ROWS = 512
QPK = 4
CH = 64

EPS_NORM = 1e-05
ROPE_BASE = 1000000.0
BETA_ONE = 0.5
BETA_TWO = 0.5
EPS_ADAM = 1e-06
DECAY = 0.01
RATE = 0.5
F32 = jnp.float32
BF16 = jnp.bfloat16
OFF = -1e5
VMEM_LIMIT = 50 * 1024 * 1024


def inverse_rms(array_in):
    return lax.rsqrt(jnp.mean(array_in * array_in, axis=-1, keepdims=True) + EPS_NORM)


def adapt(weight, first_old, second_old, grad_in):
    first_new = BETA_ONE * first_old + (1.0 - BETA_ONE) * grad_in
    second_new = BETA_TWO * second_old + (1.0 - BETA_TWO) * grad_in * grad_in
    direction = (
        first_new
        / (1.0 - BETA_ONE**STEP)
        / (jnp.sqrt(second_new / (1.0 - BETA_TWO**STEP)) + EPS_ADAM)
        + DECAY * weight
    )
    return (first_new, second_new, direction)


def perm_x(k):
    return [(i, (i // 4) * 4 + (i % 4 - k) % 4) for i in range(16)]


def perm_y(k):
    return [(i, ((i // 4 - k) % 4) * 4 + i % 4) for i in range(16)]


def perm_z(k):
    return [(i, ((i // 2 - k) % 4) * 2 + i % 2) for i in range(8)]


PERM_CORE = [(i, i ^ 1) for i in range(8)]


def from_x(a, k):
    return lax.ppermute(a, "dp", perm_x(k))


def from_y(a, k):
    return lax.ppermute(a, "dp", perm_y(k))


def from_z(a, k):
    return lax.ppermute(a, "tensor", perm_z(k))


def from_core(a):
    return lax.ppermute(a, "tensor", PERM_CORE)


def gather_dp(a):
    row = jnp.stack([a] + [from_x(a, k) for k in (1, 2, 3)])
    return [row] + [from_y(row, k) for k in (1, 2, 3)]


def scatter_dp(groups):
    got = [None] + [from_y(groups[k].astype(BF16), -k) for k in (1, 2, 3)]
    row = (groups[0].astype(F32) + got[2].astype(F32)) + (got[1].astype(F32) + got[3].astype(F32))
    low = row.astype(BF16)
    back = [None] + [from_x(low[k], -k) for k in (1, 2, 3)]
    return (row[0] + back[2].astype(F32)) + (back[1].astype(F32) + back[3].astype(F32))


def scatter_tensor(near, far):
    near = near.astype(F32) + from_core(far.astype(BF16)).astype(F32)
    parts = near.reshape(4, CH, near.shape[-1])
    low = parts.astype(BF16)
    got = [None] + [from_z(low[k], -k) for k in (1, 2, 3)]
    return (parts[0] + got[2].astype(F32)) + (got[1].astype(F32) + got[3].astype(F32))


def gather_tensor(a):
    near = jnp.concatenate([a] + [from_z(a, k) for k in (1, 2, 3)], axis=0)
    return near, from_core(near)


def sum_all(a):
    for step in (from_x, from_y, from_z):
        a = (a + step(a, 2)) + (step(a, 1) + step(a, 3))
    return a + from_core(a)


def params(vmem=VMEM_LIMIT):
    return pltpu.CompilerParams(vmem_limit_bytes=vmem)


def prepare_kernel(row_ref, col_ref, tok_ref, cot_ref, gain_ref, out_ref, dy_ref):
    x = tok_ref[...].astype(F32)
    scale = inverse_rms(x)
    normed = (x * scale * gain_ref[...]).astype(BF16)
    for slot in range(16):
        at = pl.multiple_of(col_ref[slot] * 128, 128)
        out_ref[:, pl.ds(at, 128)] = normed[:, slot * 128 : (slot + 1) * 128]
    dy_ref[...] = cot_ref[...]


def prepare(row_table, slot_of, tokens, cotangent, gain):
    return pl.pallas_call(
        prepare_kernel,
        grid_spec=pltpu.PrefetchScalarGridSpec(
            num_scalar_prefetch=2,
            grid=(8,),
            in_specs=[
                pl.BlockSpec((CH, D), lambda i, r, c: (r[i], 0)),
                pl.BlockSpec((CH, D), lambda i, r, c: (r[i], 0)),
                pl.BlockSpec((1, D), lambda i, r, c: (0, 0)),
            ],
            out_specs=[
                pl.BlockSpec((CH, D), lambda i, r, c: (i, 0)),
                pl.BlockSpec((CH, D), lambda i, r, c: (i, 0)),
            ],
        ),
        out_shape=[
            jax.ShapeDtypeStruct((ROWS, D), BF16),
            jax.ShapeDtypeStruct((ROWS, D), BF16),
        ],
        compiler_params=params(),
        name="prepare",
    )(row_table, slot_of, tokens, cotangent, gain)


def lane_of(shape):
    return lax.broadcasted_iota(jnp.int32, shape, len(shape) - 1)


def head_sums(a, low_half):
    left = jnp.sum(jnp.where(low_half, a, 0.0), axis=-1, keepdims=True)
    right = jnp.sum(jnp.where(low_half, 0.0, a), axis=-1, keepdims=True)
    return jnp.where(low_half, left, right)


def turn(a, first):
    return jnp.where(first, pltpu.roll(a, 96, 1), pltpu.roll(a, 32, 1))


def project_kernel(x_ref, w0, w1, w2, w3, cos_ref, sin_ref, gain_ref, proj_ref, q_ref, kv_ref):
    acc = None
    for group, ref in enumerate((w0, w1, w2, w3)):
        for j in range(4):
            slot = group * 4 + j
            term = jnp.dot(
                x_ref[:, slot * 128 : (slot + 1) * 128],
                ref[j, :128, :],
                preferred_element_type=F32,
            )
            acc = term if acc is None else acc + term
    proj_ref[...] = acc
    lane = lane_of((x_ref.shape[0], 128))
    low_half = lane < 64
    first = (lane & 63) < 32
    cosine = cos_ref[...]
    sine = jnp.where(first, -sin_ref[...], sin_ref[...])
    for pair in range(3):
        u = acc[:, pair * 128 : (pair + 1) * 128]
        scale = lax.rsqrt(head_sums(u * u, low_half) * (1.0 / HD) + EPS_NORM)
        hat = u * scale * gain_ref[pair // 2 : pair // 2 + 1, :]
        turned = hat * cosine + turn(hat, first) * sine
        if pair < 2:
            q_ref[:, pair * 128 : (pair + 1) * 128] = (turned.astype(BF16).astype(F32) * 0.125).astype(BF16)
        else:
            kv_ref[...] = jnp.where(low_half, turned, u).astype(BF16)


def project(x, w_groups, cosine, sine, gains):
    tile = 128
    wspec = pl.BlockSpec((4, 144, 384), lambda i: (0, 0, 0))
    return pl.pallas_call(
        project_kernel,
        grid=(ROWS // tile,),
        in_specs=[pl.BlockSpec((tile, D), lambda i: (i, 0))]
        + [wspec] * 4
        + [
            pl.BlockSpec((tile, 128), lambda i: (i, 0)),
            pl.BlockSpec((tile, 128), lambda i: (i, 0)),
            pl.BlockSpec((8, 128), lambda i: (0, 0)),
        ],
        out_specs=[
            pl.BlockSpec((tile, 384), lambda i: (i, 0)),
            pl.BlockSpec((tile, 256), lambda i: (i, 0)),
            pl.BlockSpec((tile, 128), lambda i: (i, 0)),
        ],
        out_shape=[
            jax.ShapeDtypeStruct((ROWS, 384), F32),
            jax.ShapeDtypeStruct((ROWS, 256), BF16),
            jax.ShapeDtypeStruct((ROWS, 128), BF16),
        ],
        compiler_params=params(),
        name="project",
    )(x, *w_groups, cosine, sine, gains)


def lane_masks():
    low = (lane_of((1, 128)) < 64).astype(F32)
    return low.astype(BF16), (1.0 - low).astype(BF16)


def allowed_keys(is_own, kinfo_ref, qinfo_ref):
    own_seg = kinfo_ref[:, 0:1]
    first_seg = kinfo_ref[:, 1:2]
    pos = kinfo_ref[:, 2:3]
    seg = jnp.where(is_own, own_seg, first_seg)
    pos = jnp.where(is_own, pos, -1)
    return (seg == qinfo_ref[0:1, :]) & (pos <= qinfo_ref[1:2, :])


def forward_kernel(
    blk_ref, q_ref, kv0, kv1, kv2, kv3, kinfo_ref, qinfo_ref, bias_ref,
    mixed_ref, out_ref, lse_ref, kv_all, q_t, acc,
):
    for group, ref in enumerate((kv0, kv1, kv2, kv3)):
        kv_all[group * 4 : (group + 1) * 4] = ref[...]
    acc[...] = jnp.zeros_like(acc)
    turned = q_ref[...].astype(F32).T
    row = lax.broadcasted_iota(jnp.int32, (64, ROWS), 0)
    bias = jnp.where(row == 0, bias_ref[...], 0.0).astype(BF16)
    for head in range(QPK):
        q_t[head, :64, :] = turned[head * 64 : (head + 1) * 64, :].astype(BF16)
        q_t[head, 64:, :] = bias
    keep_k, keep_v = lane_masks()
    me = blk_ref[16]

    def step(slot, carry):
        block = blk_ref[slot]

        def work(masked):
            kv = kv_all[slot]
            keys = kv * keep_k + (keep_v if not masked else jnp.zeros_like(keep_v))
            vals = (kv * keep_v + keep_k).astype(F32).T.astype(BF16)
            allowed = allowed_keys(block == me, kinfo_ref, qinfo_ref) if masked else None
            for head in range(QPK):
                scores = jnp.dot(keys, q_t[head], preferred_element_type=F32)
                probs = jnp.exp(scores)
                if masked:
                    probs = jnp.where(allowed, probs, 0.0)
                acc[head] += jnp.dot(vals, probs.astype(BF16), preferred_element_type=F32)

        @pl.when((block == 0) | (block == me))
        def _():
            work(True)

        @pl.when((block > 0) & (block < me))
        def _():
            work(False)

        return carry

    lax.fori_loop(0, 16, step, 0)
    heads = []
    for head in range(QPK):
        total = acc[head, 0:1, :]
        heads.append(acc[head, 64:, :] / total)
        lse_ref[head : head + 1, :] = jnp.log(total)
    lse_ref[QPK:, :] = jnp.zeros((8 - QPK, ROWS), F32)
    out = jnp.concatenate(heads, axis=0).T
    out_ref[...] = out
    mixed_ref[...] = out.astype(BF16)


def attend(blocks, q, kv_groups, kinfo, qinfo, bias):
    vm = pl.BlockSpec(memory_space=pltpu.VMEM)
    return pl.pallas_call(
        forward_kernel,
        in_specs=[pl.BlockSpec(memory_space=pltpu.SMEM)] + [vm] * 8,
        out_specs=[vm] * 3,
        out_shape=[
            jax.ShapeDtypeStruct((ROWS, 256), BF16),
            jax.ShapeDtypeStruct((ROWS, 256), F32),
            jax.ShapeDtypeStruct((8, ROWS), F32),
        ],
        scratch_shapes=[
            pltpu.VMEM((16, ROWS, 128), BF16),
            pltpu.VMEM((QPK, 128, ROWS), BF16),
            pltpu.VMEM((QPK, 128, ROWS), F32),
        ],
        compiler_params=params(),
        name="attend",
    )(blocks, q, *kv_groups, kinfo, qinfo, bias)


def three_rows(row, value, at):
    high = value.astype(BF16).astype(F32)
    rest = value - high
    middle = rest.astype(BF16).astype(F32)
    low = rest - middle
    return (
        jnp.where(row == at, high, 0.0)
        + jnp.where(row == at + 1, middle, 0.0)
        + jnp.where(row == at + 2, low, 0.0)
    )


def backward_kernel(
    blk_ref, q_ref, do_ref, out_ref, lse_ref, kv0, kv1, kv2, kv3, kinfo_ref, qinfo_ref, bias_ref,
    dq_ref, dkv_ref, kv_all, q_t, do_t, q_pad, do_pad, dq_t,
):
    for group, ref in enumerate((kv0, kv1, kv2, kv3)):
        kv_all[group * 4 : (group + 1) * 4] = ref[...]
    dq_t[...] = jnp.zeros_like(dq_t)
    q = q_ref[...].astype(F32)
    do = do_ref[...].astype(F32)
    q_turned = q.T
    do_turned = do.T
    dots = (do * out_ref[...]).T
    row = lax.broadcasted_iota(jnp.int32, (64, ROWS), 0)
    low_half = lane_of((ROWS, 128)) < 64
    for head in range(QPK):
        at = slice(head * 64, (head + 1) * 64)
        delta = jnp.sum(dots[at, :], axis=0, keepdims=True)
        extra = three_rows(row, -lse_ref[head : head + 1, :], 0)
        extra = extra + jnp.where(row == 3, bias_ref[...], 0.0)
        q_t[head, :64, :] = q_turned[at, :].astype(BF16)
        q_t[head, 64:, :] = extra.astype(BF16)
        do_t[head, :64, :] = three_rows(row, -delta, 0).astype(BF16)
        do_t[head, 64:, :] = do_turned[at, :].astype(BF16)
        pair = slice((head // 2) * 128, (head // 2 + 1) * 128)
        q_head = q[:, pair]
        do_head = do[:, pair]
        if head % 2:
            q_head = pltpu.roll(q_head, 64, 1)
        else:
            do_head = pltpu.roll(do_head, 64, 1)
        q_pad[head] = jnp.where(low_half, q_head, 0.0).astype(BF16)
        do_pad[head] = jnp.where(low_half, 0.0, do_head).astype(BF16)
    keep_k, keep_v = lane_masks()
    me = blk_ref[16]

    def step(slot, carry):
        block = blk_ref[slot]

        def work(masked):
            kv = kv_all[slot]
            keys = kv * keep_k + keep_v
            vals = kv * keep_v + keep_k
            keys_turned = kv.astype(F32).T[:64, :].astype(BF16)
            allowed = allowed_keys(block == me, kinfo_ref, qinfo_ref) if masked else None
            total = None
            for head in range(QPK):
                q_t_head = q_t[head]
                if masked:
                    q_t_head = jnp.where(
                        lax.broadcasted_iota(jnp.int32, (128, ROWS), 0) == 67, 0.0, q_t_head.astype(F32)
                    ).astype(BF16)
                scores = jnp.dot(keys, q_t_head, preferred_element_type=F32)
                probs = jnp.exp(scores)
                if masked:
                    probs = jnp.where(allowed, probs, 0.0)
                grads = jnp.dot(vals, do_t[head], preferred_element_type=F32)
                grads = (probs * grads).astype(BF16)
                term = jnp.dot(probs.astype(BF16), do_pad[head], preferred_element_type=F32)
                term = term + jnp.dot(grads, q_pad[head], preferred_element_type=F32)
                total = term if total is None else total + term
                dq_t[head * 64 : (head + 1) * 64, :] += jnp.dot(
                    keys_turned, grads, preferred_element_type=F32
                )
            dkv_ref[slot] = total.astype(BF16)

        @pl.when((block == 0) | (block == me))
        def _():
            work(True)

        @pl.when((block > 0) & (block < me))
        def _():
            work(False)

        @pl.when(block > me)
        def _():
            dkv_ref[slot] = jnp.zeros((ROWS, 128), BF16)

        return carry

    lax.fori_loop(0, 16, step, 0)
    dq_ref[...] = (dq_t[...].T * 0.125).astype(BF16)


def attend_back(blocks, q, do, out, lse, kv_groups, kinfo, qinfo, bias):
    vm = pl.BlockSpec(memory_space=pltpu.VMEM)
    return pl.pallas_call(
        backward_kernel,
        in_specs=[pl.BlockSpec(memory_space=pltpu.SMEM)] + [vm] * 11,
        out_specs=[vm] * 2,
        out_shape=[
            jax.ShapeDtypeStruct((ROWS, 256), BF16),
            jax.ShapeDtypeStruct((16, ROWS, 128), BF16),
        ],
        scratch_shapes=[
            pltpu.VMEM((16, ROWS, 128), BF16),
            pltpu.VMEM((QPK, 128, ROWS), BF16),
            pltpu.VMEM((QPK, 128, ROWS), BF16),
            pltpu.VMEM((QPK, ROWS, 128), BF16),
            pltpu.VMEM((QPK, ROWS, 128), BF16),
            pltpu.VMEM((256, ROWS), F32),
        ],
        compiler_params=params(),
        name="attend_back",
    )(blocks, q, do, out, lse, *kv_groups, kinfo, qinfo, bias)


def heads_back_kernel(proj_ref, grad_ref, cos_ref, sin_ref, gain_ref, out_ref, sum_ref):
    lane = lane_of((proj_ref.shape[0], 128))
    low_half = lane < 64
    first = (lane & 63) < 32
    cosine = cos_ref[...]
    sine = jnp.where(first, sin_ref[...], -sin_ref[...])
    sums = []
    for pair in range(3):
        at = slice(pair * 128, (pair + 1) * 128)
        u = proj_ref[:, at]
        grad = grad_ref[:, at].astype(F32)
        scale = lax.rsqrt(head_sums(u * u, low_half) * (1.0 / HD) + EPS_NORM)
        hat = u * scale
        turned = grad * cosine + turn(grad, first) * sine
        sums.append(jnp.sum(turned * hat, axis=0, keepdims=True))
        grad_hat = turned * gain_ref[pair // 2 : pair // 2 + 1, :]
        mean = head_sums(grad_hat * hat, low_half) * (1.0 / HD)
        back = scale * (grad_hat - hat * mean)
        if pair == 2:
            back = jnp.where(low_half, back, grad)
        out_ref[:, at] = back.astype(BF16)

    @pl.when(pl.program_id(0) == 0)
    def _():
        sum_ref[...] = jnp.zeros_like(sum_ref)

    sum_ref[0:1, :] += sums[0] + sums[1]
    sum_ref[1:2, :] += sums[2]


def heads_back(proj, grad, cosine, sine, gains):
    tile = 128
    return pl.pallas_call(
        heads_back_kernel,
        grid=(ROWS // tile,),
        in_specs=[
            pl.BlockSpec((tile, 384), lambda i: (i, 0)),
            pl.BlockSpec((tile, 384), lambda i: (i, 0)),
            pl.BlockSpec((tile, 128), lambda i: (i, 0)),
            pl.BlockSpec((tile, 128), lambda i: (i, 0)),
            pl.BlockSpec((8, 128), lambda i: (0, 0)),
        ],
        out_specs=[
            pl.BlockSpec((tile, 384), lambda i: (i, 0)),
            pl.BlockSpec((8, 128), lambda i: (0, 0)),
        ],
        out_shape=[
            jax.ShapeDtypeStruct((ROWS, 384), BF16),
            jax.ShapeDtypeStruct((8, 128), F32),
        ],
        compiler_params=params(),
        name="heads_back",
    )(proj, grad, cosine, sine, gains)


def norm_back(grad_in, normed, inv_scale, gain):
    grad_hat = grad_in * gain
    return inv_scale * (grad_hat - normed * jnp.mean(grad_hat * normed, axis=-1, keepdims=True))


def dot_cols(a, b):
    return lax.dot_general(a, b, (((1,), (1,)), ((), ())), preferred_element_type=F32)


def dot_rows(a, b):
    return lax.dot_general(a, b, (((0,), (0,)), ((), ())), preferred_element_type=F32)


def dot(a, b):
    return jnp.dot(a, b, preferred_element_type=F32)


def local(
    tokens,
    segments,
    weight_qkv,
    weight_out,
    weight_gate_up,
    weight_down,
    norm_gains,
    head_gains,
    first_qkv,
    first_out,
    first_gate_up,
    first_down,
    first_norm,
    first_head,
    second_qkv,
    second_out,
    second_gate_up,
    second_down,
    second_norm,
    second_head,
    cotangent,
):
    dp = lax.axis_index("dp")
    tensor = lax.axis_index("tensor")
    y, x = dp // 4, dp % 4
    z, core = tensor // 2, tensor % 2
    slots = jnp.arange(8, dtype=jnp.int32)
    row_table = 2 * ((z + slots % 4) % 4) + (core ^ (slots // 4))
    near_z = (jnp.arange(4, dtype=jnp.int32) + y) % 4
    near_x = (jnp.arange(4, dtype=jnp.int32) + x) % 4
    blocks = (near_z[:, None] * 4 + near_x[None, :]).reshape(16)
    back_y = (jnp.arange(4, dtype=jnp.int32) - y) % 4
    back_x = (jnp.arange(4, dtype=jnp.int32) - x) % 4
    slot_of = (back_y[:, None] * 4 + back_x[None, :]).reshape(16)
    token_ids = (row_table[:, None] * CH + jnp.arange(CH, dtype=jnp.int32)[None, :]).reshape(ROWS)
    seg_rows = jnp.concatenate(
        [lax.dynamic_slice_in_dim(segments, row_table[j] * CH, CH, 0) for j in range(8)]
    )

    seg_low = jnp.stack([seg_rows // 64, seg_rows % 64]).astype(BF16).reshape(4, 256)
    seg_low = jnp.pad(seg_low, ((0, 12), (0, 128)))
    qkv_groups = gather_dp(jnp.concatenate([weight_qkv.astype(BF16), seg_low], axis=0))

    full_out = lax.all_gather(weight_out.T.astype(BF16), "dp", axis=0, tiled=True)
    full_down = lax.all_gather(weight_down.T.astype(BF16), "dp", axis=0, tiled=True)
    full_gate_up = lax.all_gather(
        jnp.concatenate([weight_gate_up[0], weight_gate_up[1]], axis=1).astype(BF16),
        "dp",
        axis=0,
        tiled=True,
    )

    attn_in, dy = prepare(row_table, slot_of, tokens, cotangent, norm_gains[0:1])
    frequency = ROPE_BASE ** (-(jnp.arange(HD // 2, dtype=F32) * 2.0 / HD))
    angles = (dp * ROWS + token_ids).astype(F32)[:, None] * jnp.tile(frequency, 4)[None, :]
    cosine, sine = jnp.cos(angles), jnp.sin(angles)
    ones = jnp.ones((1, HD), F32)
    gain_rows = jnp.concatenate(
        [
            jnp.concatenate([head_gains[0:1], head_gains[0:1]], axis=1),
            jnp.concatenate([head_gains[1:2], ones], axis=1),
            jnp.zeros((6, 128), F32),
        ]
    )
    projected, queries, local_kv = project(attn_in, qkv_groups, cosine, sine, gain_rows)
    kv_groups = gather_dp(local_kv)

    qkv_slots = jnp.stack(qkv_groups)
    first_seg = lax.dynamic_slice(
        qkv_slots, (back_y[0], back_x[0], 128, 0), (1, 1, 4, 256)
    ).astype(jnp.int32).reshape(2, ROWS)
    first_seg = first_seg[0] * 64 + first_seg[1]
    pair = jnp.concatenate([qkv_slots, qkv_slots])
    pair = lax.dynamic_slice(pair, (back_y[0], 0, 0, 0), (4, 4, 128, 384))
    pair = jnp.concatenate([pair, pair], axis=1)
    full_qkv = lax.dynamic_slice(pair, (0, back_x[0], 0, 0), (4, 4, 128, 384)).reshape(D, 384)

    kinfo = jnp.stack([seg_rows, first_seg, token_ids], axis=1)
    qinfo = jnp.concatenate([seg_rows[None], token_ids[None], jnp.zeros((6, ROWS), jnp.int32)])
    bias = jnp.where(seg_rows == segments[0], 0.0, OFF).astype(F32)[None]
    block_info = jnp.concatenate([blocks, dp[None]]).astype(jnp.int32)
    mixed, attn_f, log_total = attend(block_info, queries, kv_groups, kinfo, qinfo, bias)

    far = dot_cols(mixed[256:], full_out)
    near = dot_cols(mixed[:256], full_out)
    own_tokens = lax.dynamic_slice_in_dim(tokens, tensor * CH, CH, 0).astype(F32)
    hidden_one = own_tokens + scatter_tensor(near, far)
    scale_two = inverse_rms(hidden_one)
    normed_two = hidden_one * scale_two
    ffn_in = jnp.concatenate(gather_tensor((normed_two * norm_gains[1]).astype(BF16)), axis=0)

    gate_up = dot(ffn_in, full_gate_up)
    gate_value, up_value = gate_up[:, :1024], gate_up[:, 1024:]
    sigmoid_gate = jax.nn.sigmoid(gate_value)
    activated = gate_value * sigmoid_gate
    inner_act = (activated * up_value).astype(BF16)
    grad_inner = dot(dy, full_down)
    grad_gate = (
        grad_inner * up_value * sigmoid_gate * (1.0 + gate_value * (1.0 - sigmoid_gate))
    ).astype(BF16)
    grad_up = (grad_inner * activated).astype(BF16)
    grad_both = jnp.concatenate([grad_gate, grad_up], axis=1)
    far = dot_cols(grad_both[256:], full_gate_up)
    near = dot_cols(grad_both[:256], full_gate_up)
    grad_ffn_in = scatter_tensor(near, far)

    grad_down = lax.psum_scatter(
        dot_rows(dy, inner_act).astype(BF16), "dp", scatter_dimension=0, tiled=True
    )
    grad_gate_up = lax.psum_scatter(
        dot_rows(ffn_in, grad_both).astype(BF16), "dp", scatter_dimension=0, tiled=True
    )
    ffn_part = dot_cols(inner_act, full_down).astype(BF16)
    ffn_part = jnp.concatenate(
        [ffn_part[at * CH : (at + 1) * CH] for at in range(8)]
    )

    own_dy = dy[:CH].astype(F32)
    gain_ffn = jnp.sum(grad_ffn_in * normed_two, axis=0)
    grad_hidden = own_dy + norm_back(grad_ffn_in, normed_two, scale_two, norm_gains[1])
    grad_attn = jnp.concatenate(gather_tensor(grad_hidden.astype(BF16)), axis=0)
    grad_mixed = dot(grad_attn, full_out).astype(BF16)
    grad_out_w = lax.psum_scatter(
        dot_rows(grad_attn, mixed).astype(BF16), "dp", scatter_dimension=0, tiled=True
    )
    grad_query, grad_kv = attend_back(
        block_info, queries, grad_mixed, attn_f, log_total, kv_groups, kinfo, qinfo, bias
    )
    grad_kv = scatter_dp([grad_kv[k * 4 : (k + 1) * 4] for k in range(4)]).astype(BF16)
    grad_projected, gain_heads = heads_back(
        projected, jnp.concatenate([grad_query, grad_kv], axis=1), cosine, sine, gain_rows
    )
    grad_qkv = dot_rows(attn_in, grad_projected).astype(BF16).reshape(4, 4, 128, 384)
    grad_qkv = scatter_dp([grad_qkv[k] for k in range(4)])
    far = dot_cols(grad_projected[256:], full_qkv)
    near = dot_cols(grad_projected[:256], full_qkv)
    grad_attn_in = scatter_tensor(near, far)
    scale_one = inverse_rms(own_tokens)
    normed_one = own_tokens * scale_one
    gain_attn = jnp.sum(grad_attn_in * normed_one, axis=0)
    input_grad = (
        grad_hidden + norm_back(grad_attn_in, normed_one, scale_one, norm_gains[0])
    ).astype(BF16)

    ffn_total = scatter_tensor(ffn_part[:256], ffn_part[256:])
    block_out = (hidden_one + ffn_total).astype(BF16)

    def in_place(parts):
        rows = jnp.concatenate(parts, axis=0).reshape(2, 4, CH, D)
        twice = jnp.concatenate([rows, rows], axis=1)
        rows = lax.dynamic_slice(twice, (0, (4 - z) % 4, 0, 0), (2, 4, CH, D))
        rows = jnp.where(core == 0, rows, rows[::-1])
        return rows.transpose(1, 0, 2, 3).reshape(ROWS, D)

    block_out = in_place(gather_tensor(block_out))
    input_grad = in_place(gather_tensor(input_grad))

    matrices = (
        (weight_qkv, first_qkv, second_qkv, grad_qkv),
        (weight_out, first_out, second_out, grad_out_w.astype(F32).T),
        (
            weight_gate_up,
            first_gate_up,
            second_gate_up,
            jnp.stack([grad_gate_up[:, :1024], grad_gate_up[:, 1024:]]).astype(F32),
        ),
        (weight_down, first_down, second_down, grad_down.astype(F32).T),
    )
    adapted = [adapt(*entry) for entry in matrices]
    squares = jnp.stack(
        [jnp.sum(entry[0] * entry[0]) for entry in matrices]
        + [jnp.sum(item[2] * item[2]) for item in adapted]
    )
    sums = jnp.concatenate(
        [
            gain_attn.reshape(16, 128),
            gain_ffn.reshape(16, 128),
            gain_heads,
            jnp.pad(squares, (0, 120))[None],
            jnp.zeros((7, 128), F32),
        ]
    )
    sums = sum_all(sums)
    gain_norm_grad = sums[:32].reshape(2, D)
    gain_head_grad = jnp.stack([sums[32, :HD] + sums[32, HD:], sums[33, :HD]])
    square_sums = sums[40, :8]
    weight_norms = [jnp.sqrt(square_sums[index]) for index in range(4)]
    step_norms = [jnp.sqrt(square_sums[4 + index]) for index in range(4)]
    gain_sets = (
        (norm_gains, first_norm, second_norm, gain_norm_grad),
        (head_gains, first_head, second_head, gain_head_grad),
    )
    for entry in gain_sets:
        first_new, second_new, direction = adapt(entry[0], entry[1], entry[2], entry[3])
        adapted.append((first_new, second_new, direction))
        weight_norms.append(jnp.sqrt(jnp.sum(entry[0] * entry[0])))
        step_norms.append(jnp.sqrt(jnp.sum(direction * direction)))
    params_in = (weight_qkv, weight_out, weight_gate_up, weight_down, norm_gains, head_gains)
    ratios = [weight_norms[index] / (step_norms[index] + EPS_ADAM) for index in range(6)]
    new_params = [params_in[index] - RATE * ratios[index] * adapted[index][2] for index in range(6)]
    trust_stats = jnp.stack([jnp.stack(weight_norms), jnp.stack(step_norms), jnp.stack(ratios)])
    return (
        block_out,
        input_grad,
        *new_params,
        *[item[0] for item in adapted],
        *[item[1] for item in adapted],
        trust_stats,
    )


def solution(mesh):
    matrix_specs = (P("dp", "tensor"), P("tensor", "dp"), P(None, "dp", "tensor"), P("tensor", "dp"), P(), P())
    in_specs = (P("dp", None), P("dp"), *matrix_specs, *matrix_specs, *matrix_specs, P("dp", None))
    out_specs = (P("dp", None), P("dp", None), *matrix_specs, *matrix_specs, *matrix_specs, P())
    return jax.shard_map(local, mesh=mesh, in_specs=in_specs, out_specs=out_specs, check_vma=False)
```

time: 1540 us -> 618 us (0.40)
  waiting for transfers between devices: 896 us -> 253 us
  local copies, waits for them, and re-layouts: 356 us -> 52.9 us
  starting transfers between devices: 1.62 us -> 146 us
  blocking collectives: 84 us -> 0 us
  other arithmetic: 86.2 us -> 50 us
  matrix products: 79.1 us -> 51 us
  Pallas kernels: 0 us -> 24.3 us
    unnamed x136 -> x130, local copies, waits for them, and re-layouts: 343 us -> 31.8 us
    unnamed x16 -> x6, waiting for transfers between devices: 282 us -> 0.1 us
    psum x3 -> x0, waiting for transfers between devices: 233 us -> none  [the longest x1 96.7 us: local(): lax.psum(jnp.dot(mixed, full_out, preferred_element_type=jnp.float32).ast...]
    all_gather x5 -> x3, waiting for transfers between devices: 224 us -> 42.6 us  [the longest x1 42.6 us: local(): lax.all_gather(weight_down.T.astype(BF16), 'dp', axis=0, tiled=True)]
    ppermute x0 -> x66, waiting for transfers between devices: none -> 178 us  [the longest x15 99.4 us: from_y(): return lax.ppermute(a, 'dp', perm_y(k))]
    ppermute x0 -> x66, starting transfers between devices: none -> 146 us  [the longest x15 49.9 us: from_y(): return lax.ppermute(a, 'dp', perm_y(k))]
    reduce_scatter x2 -> x3, waiting for transfers between devices: 157 us -> 32.8 us  [the longest x1 32.7 us: local(): lax.psum_scatter(dot_rows(ffn_in, grad_both).astype(BF16), 'dp', scatter_...]
    psum x1 -> x0, blocking collectives: 66.5 us -> none  [local(): lax.psum((jnp.stack([gain_attn_part, gain_ffn_part]), jnp.stack([gain_que...]
  transfers between devices with their start and end apart: 13 -> 72, of which waited for: 13 -> 38; matrix products, arithmetic and copies ran while one was open for 8% -> 18% of each run, Pallas kernels for 0% -> 4%
where the time goes in v1:
time: 618 us; the launch traced here: 608 us
  waiting for transfers between devices  253 us (41%)
  starting transfers between devices  146 us (24%)
  local copies, waits for them, and re-layouts  52.9 us (9%)
  matrix products  51 us (8%)
  other arithmetic  50 us (8%)
  between operations  29.9 us (5%)
  Pallas kernels  24.3 us (4%)
    ppermute x15, waiting for transfers between devices, from_y(): return lax.ppermute(a, 'dp', perm_y(k))  99.4 us
    ppermute x27, waiting for transfers between devices, from_z(): return lax.ppermute(a, 'tensor', perm_z(k))  55.6 us
    ppermute x15, starting transfers between devices, from_y(): return lax.ppermute(a, 'dp', perm_y(k))  49.9 us
    all_gather x1, waiting for transfers between devices, local(): lax.all_gather(weight_down.T.astype(BF16), 'dp', axis=0, tiled=True)  42.6 us
    ppermute x27, starting transfers between devices, from_z(): return lax.ppermute(a, 'tensor', perm_z(k))  36.1 us
    reduce_scatter x1, waiting for transfers between devices, local(): lax.psum_scatter(dot_rows(ffn_in, grad_both).astype(BF16), 'dp', scatter_...  32.7 us
    unnamed x130, local copies, waits for them, and re-layouts  31.8 us
    ppermute x15, starting transfers between devices, from_x(): return lax.ppermute(a, 'dp', perm_x(k))  31.4 us
  transfers between devices with their start and end apart: 72, of which 38 were waited for; matrix products, arithmetic and copies ran while one was open for 18% of the time, Pallas kernels for 4%

profile of v1, /device:TPU:1, one launch (start us, length us, event | category | flops | bytes accessed | tf_op | source)
XLA Modules:
  0.0 608.1 jit_solution(8617021581024474758)
XLA Ops:
  27.1 6.8 %prepare.1 = (bf16[512,2048]{1,0:T(8,128)(2,1)S(1)}, bf16[512,2048]{1,0:T(8,128)(2,1)}) custom-call(s32[8]{0:T(128)S(1)} %get-tuple-element.151.row_ref, s32[16]{0:T(128)S(1)} %add.562.col_ref, bf16[512,2048]{1,0:T(8,128)(2,1)} %tok_ref.1, bf16[512,2048]{1,0:T(8,128)(2,1)} %cot_ref.1, f32[1,2048]{1,0:T(1,128)S(1)} %get-tuple-element.211.gain_ref), custom_call_target="tpu_custom_call" | custom-call | tf_op jit(solution)/shard_map/prepare/pallas_call | solution.py:126
  40.9 8.4 %collective-permute-done.3.w1 = bf16[4,144,384]{2,1,0:T(8,128)(2,1)S(1)} collective-permute-done((bf16[4,144,384]{2,1,0:T(8,128)(2,1)S(1)}, bf16[4,144,384]{2,1,0:T(8,128)(2,1)S(1)}, u32[]{:S(2)}, u32[]{:S(2)}) %collective-permute-start.3) | collective-permute-done | bytes 442400 | tf_op jit(solution)/shard_map/ppermute | solution.py:68
  51.7 14.4 %collective-permute-done.5.w3 = bf16[4,144,384]{2,1,0:T(8,128)(2,1)S(1)} collective-permute-done((bf16[4,144,384]{2,1,0:T(8,128)(2,1)S(1)}, bf16[4,144,384]{2,1,0:T(8,128)(2,1)S(1)}, u32[]{:S(2)}, u32[]{:S(2)}) %collective-permute-start.5) | collective-permute-done | bytes 442400 | tf_op jit(solution)/shard_map/ppermute | solution.py:68
  74.3 5.3 collective-permute-done.8
  81.7 19.1 %collective-permute-done.9.kv1 = bf16[4,512,128]{2,1,0:T(8,128)(2,1)S(1)} collective-permute-done((bf16[4,512,128]{2,1,0:T(8,128)(2,1)S(1)}, bf16[4,512,128]{2,1,0:T(8,128)(2,1)S(1)}, u32[]{:S(2)}, u32[]{:S(2)}) %collective-permute-start.9) | collective-permute-done | bytes 524320 | tf_op jit(solution)/shard_map/ppermute | solution.py:68
  100.8 13.9 %collective-permute-done.11.kv3 = bf16[4,512,128]{2,1,0:T(8,128)(2,1)} collective-permute-done((bf16[4,512,128]{2,1,0:T(8,128)(2,1)S(1)}, bf16[4,512,128]{2,1,0:T(8,128)(2,1)}, u32[]{:S(2)}, u32[]{:S(2)}) %collective-permute-start.11) | collective-permute-done | bytes 524320 | tf_op jit(solution)/shard_map/ppermute | solution.py:68
  132.1 9.4 %collective-permute-done.15 = bf16[64,2048]{1,0:T(8,128)(2,1)} collective-permute-done((bf16[64,2048]{1,0:T(8,128)(2,1)}, bf16[64,2048]{1,0:T(8,128)(2,1)}, u32[]{:S(2)}, u32[]{:S(2)}) %collective-permute-start.15) | collective-permute-done | bytes 262176 | tf_op jit(solution)/shard_map/ppermute | solution.py:72
  156.4 7.4 %collective-permute-done.18 = bf16[64,2048]{1,0:T(8,128)(2,1)S(1)} collective-permute-done((bf16[64,2048]{1,0:T(8,128)(2,1)S(1)}, bf16[64,2048]{1,0:T(8,128)(2,1)S(1)}, u32[]{:S(2)}, u32[]{:S(2)}) %collective-permute-start.18) | collective-permute-done | bytes 262176 | tf_op jit(solution)/shard_map/ppermute | solution.py:72
  167.9 10.5 %fusion.105 = f32[512,2048]{1,0:T(8,128)} fusion(bf16[512,2048]{1,0:T(8,128)(2,1)} %constant_dynamic-update-slice_fusion, bf16[2048,2048]{1,0:T(8,128)(2,1)} %all-gather.6.cloned.1.call-done), kind=kOutput, calls=%fused_computation.277 | convolution fusion | flops 4294967296 | bytes 14680064 | tf_op jit(solution)/shard_map/dot_general | solution.py:495
  178.4 42.6 %all-gather.8.cloned.1.call-done = bf16[2048,1024]{0,1:T(8,128)(2,1)} async-done(((bf16[128,1024]{0,1:T(8,128)(2,1)}), bf16[2048,1024]{0,1:T(8,128)(2,1)}) %all-gather.8.cloned.1.call-update) | async-done | bytes 4194320 | tf_op jit(solution)/shard_map/all_gather | solution.py:543
  220.9 8.2 %multiply_convert_fusion = (bf16[512,1024]{1,0:T(8,128)(2,1)S(1)}, bf16[512,1024]{1,0:T(8,128)(2,1)S(1)}, bf16[512,1024]{1,0:T(8,128)(2,1)}) fusion(f32[512,2048]{1,0:T(8,128)} %fusion.105, bf16[512,2048]{1,0:T(8,128)(2,1)} %get-tuple-element.37, bf16[2048,1024]{0,1:T(8,128)(2,1)} %all-gather.8.cloned.1.call-done), kind=kOutput, calls=%fused_computation.28 | convolution fusion | flops 2155347968 | bytes 13631488 | tf_op jit(solution)/shard_map/dot_general | solution.py:495
  242.6 9.1 %collective-permute-done.31 = bf16[64,2048]{1,0:T(8,128)(2,1)S(1)} collective-permute-done((bf16[64,2048]{1,0:T(8,128)(2,1)S(1)}, bf16[64,2048]{1,0:T(8,128)(2,1)S(1)}, u32[]{:S(2)}, u32[]{:S(2)}) %collective-permute-start.31) | collective-permute-done | bytes 262176 | tf_op jit(solution)/shard_map/ppermute | solution.py:72
  265.0 7.5 %collective-permute-done.34 = bf16[64,2048]{1,0:T(8,128)(2,1)S(1)} collective-permute-done((bf16[64,2048]{1,0:T(8,128)(2,1)S(1)}, bf16[64,2048]{1,0:T(8,128)(2,1)S(1)}, u32[]{:S(2)}, u32[]{:S(2)}) %collective-permute-start.34) | collective-permute-done | bytes 262176 | tf_op jit(solution)/shard_map/ppermute | solution.py:72
  278.6 6.2 %convolution_convert_fusion.1 = bf16[2048,1024]{1,0:T(8,128)(2,1)} fusion(bf16[512,2048]{1,0:T(8,128)(2,1)} %get-tuple-element.37, bf16[512,1024]{1,0:T(8,128)(2,1)} %get-tuple-element.156), kind=kOutput, calls=%fused_computation.5 | convolution fusion | flops 2149580800 | bytes 7340032 | tf_op jit(solution)/shard_map/dot_general | solution.py:491
  285.3 10.1 %convolution_convert_fusion = bf16[2048,2048]{1,0:T(8,128)(2,1)} fusion(bf16[512,2048]{1,0:T(8,128)(2,1)} %constant_dynamic-update-slice_fusion, bf16[512,1024]{1,0:T(8,128)(2,1)} %copy-done.47, bf16[512,1024]{1,0:T(8,128)(2,1)} %copy-done.48), kind=kOutput, calls=%fused_computation | convolution fusion | flops 4303355904 | bytes 12582912 | tf_op jit(solution)/shard_map/dot_general | solution.py:491
  311.2 6.9 %attend_back.1 = (bf16[512,256]{1,0:T(8,128)(2,1)S(1)}, bf16[16,512,128]{2,1,0:T(8,128)(2,1)}) custom-call(s32[17]{0:T(128)S(1)} %pad_add_fusion.1.blk_ref, bf16[512,256]{1,0:T(8,128)(2,1)S(1)} %get-tuple-element.34.q_ref, bf16[512,256]{1,0:T(8,128)(2,1)S(1)} %convolution_convert_fusion.8.do_ref, f32[512,256]{1,0:T(8,128)S(1)} %copy-done.5, ...), custom_call_target="tpu_custom_call" | custom-call | tf_op jit(solution)/shard_map/attend_back/pallas_call | solution.py:405
  319.5 38.1 %collective-permute-start.38 = (bf16[4,512,128]{2,1,0:T(8,128)(2,1)S(1)}, bf16[4,512,128]{2,1,0:T(8,128)(2,1)S(1)}, u32[]{:S(2)}, u32[]{:S(2)}) collective-permute-start(bf16[4,512,128]{2,1,0:T(8,128)(2,1)S(1)} %get-tuple-element.160), channel_id=1, source_target_pairs={{0,96},{8,104},{16,112},{24,120},{32,0},{40,8},{48,16},{56,24},{64... | collective-permute-start | bytes 1572872 | tf_op jit(solution)/shard_map/ppermute | solution.py:68
  359.8 25.3 %collective-permute-done.38 = bf16[4,512,128]{2,1,0:T(8,128)(2,1)S(1)} collective-permute-done((bf16[4,512,128]{2,1,0:T(8,128)(2,1)S(1)}, bf16[4,512,128]{2,1,0:T(8,128)(2,1)S(1)}, u32[]{:S(2)}, u32[]{:S(2)}) %collective-permute-start.38) | collective-permute-done | bytes 524320 | tf_op jit(solution)/shard_map/ppermute | solution.py:68
  389.3 11.7 %collective-permute-start.41 = (bf16[512,128]{1,0:T(8,128)(2,1)S(1)}, bf16[512,128]{1,0:T(8,128)(2,1)S(1)}, u32[]{:S(2)}, u32[]{:S(2)}) collective-permute-start(bf16[512,128]{1,0:T(8,128)(2,1)S(1)} %get-tuple-element.186), channel_id=1, source_target_pairs={{0,24},{8,0},{16,8},{24,16},{32,56},{40,32},{48,40},{56,48},{64,88... | collective-permute-start | bytes 393224 | tf_op jit(solution)/shard_map/ppermute | solution.py:64
  422.4 7.5 %collective-permute-done.52 = bf16[4,128,384]{2,1,0:T(8,128)(2,1)S(1)} collective-permute-done((bf16[4,128,384]{2,1,0:T(8,128)(2,1)S(1)}, bf16[4,128,384]{2,1,0:T(8,128)(2,1)S(1)}, u32[]{:S(2)}, u32[]{:S(2)}) %collective-permute-start.52) | collective-permute-done | bytes 393248 | tf_op jit(solution)/shard_map/ppermute | solution.py:68
  474.7 10.8 %collective-permute-start.27 = (bf16[256,2048]{1,0:T(8,128)(2,1)S(1)}, bf16[256,2048]{1,0:T(8,128)(2,1)S(1)}, u32[]{:S(2)}, u32[]{:S(2)}) collective-permute-start(bf16[256,2048]{1,0:T(8,128)(2,1)S(1)} %pad_maximum_fusion.3), channel_id=1, source_target_pairs={{0,1},{1,0},{2,3},{3,2},{4,5},{5,4},{6,7},{7,6},{8,9},{9,8},{10,11... | collective-permute-start | bytes 3145736 | tf_op jit(solution)/shard_map/ppermute | solution.py:76
  501.7 32.7 %reduce-scatter.6.cloned.1.call-done = bf16[128,2048]{1,0:T(8,128)(2,1)} async-done(((bf16[2048,2048]{1,0:T(8,128)(2,1)}), bf16[128,2048]{1,0:T(8,128)(2,1)}) %reduce-scatter.6.cloned.1.call-update) | async-done | bytes 524304 | tf_op jit(solution)/shard_map/reduce_scatter | solution.py:608
  539.9 5.3 stack.202
  564.5 6.8 %collective-permute-start.65 = (f32[48,128]{1,0:T(8,128)S(1)}, f32[48,128]{1,0:T(8,128)S(1)}, u32[]{:S(2)}, u32[]{:S(2)}) collective-permute-start(f32[48,128]{1,0:T(8,128)S(1)} %add_add_fusion.1), channel_id=1, source_target_pairs={{0,1},{1,0},{2,3},{3,2},{4,5},{5,4},{6,7},{7,6},{8,9},{9,8},{10,11... | collective-permute-start | bytes 73736 | tf_op jit(solution)/shard_map/ppermute | solution.py:76
  (395 shorter events, 254.2 us)
Async XLA Ops:
  7.2 112.6 %all-gather.4.cloned.1.call-start = ((), (), s32[]{:S(2)}) async-start(), calls=%async_computation.3 | async-start | bytes 1114112 | tf_op jit(solution)/shard_map/all_gather | solution.py:542
  9.5 158.4 %all-gather.6.cloned.1.call-start = ((), (), s32[]{:S(2)}) async-start(), calls=%async_computation.4 | async-start | bytes 8912896 | tf_op jit(solution)/shard_map/all_gather | solution.py:544
  11.8 209.1 %all-gather.8.cloned.1.call-start = ((), (), s32[]{:S(2)}) async-start(), calls=%async_computation.5 | async-start | bytes 4456448 | tf_op jit(solution)/shard_map/all_gather | solution.py:543
  18.1 17.2 %collective-permute-start.2 = (bf16[144,384]{1,0:T(8,128)(2,1)S(1)}, bf16[144,384]{1,0:T(8,128)(2,1)S(1)}, u32[]{:S(2)}, u32[]{:S(2)}) collective-permute-start(bf16[144,384]{1,0:T(8,128)(2,1)S(1)} %get-tuple-element.198), channel_id=1, source_target_pairs={{0,8},{8,16},{16,24},{24,0},{32,40},{40,48},{48,56},{56,32},{64,72... | collective-permute-start | bytes 331784 | tf_op jit(solution)/shard_map/ppermute | solution.py:64
  25.2 444.8 %reduce-scatter.4.cloned.1.call-start = ((), (), s32[]{:S(2)}) async-start(), calls=%async_computation.6 | async-start | bytes 1114112 | tf_op jit(solution)/shard_map/reduce_scatter | solution.py:621
  39.1 26.9 %collective-permute-start.5 = (bf16[4,144,384]{2,1,0:T(8,128)(2,1)S(1)}, bf16[4,144,384]{2,1,0:T(8,128)(2,1)S(1)}, u32[]{:S(2)}, u32[]{:S(2)}) collective-permute-start(bf16[4,144,384]{2,1,0:T(8,128)(2,1)S(1)} %get-tuple-element.191.w0), channel_id=1, source_target_pairs={{0,32},{8,40},{16,48},{24,56},{32,64},{40,72},{48,80},{56,88},{64,... | collective-permute-start | bytes 1327112 | tf_op jit(solution)/shard_map/ppermute | solution.py:68
  79.8 20.9 %collective-permute-start.9 = (bf16[4,512,128]{2,1,0:T(8,128)(2,1)S(1)}, bf16[4,512,128]{2,1,0:T(8,128)(2,1)S(1)}, u32[]{:S(2)}, u32[]{:S(2)}) collective-permute-start(bf16[4,512,128]{2,1,0:T(8,128)(2,1)S(1)} %pad_maximum_fusion.6.kv0), channel_id=1, source_target_pairs={{0,96},{8,104},{16,112},{24,120},{32,0},{40,8},{48,16},{56,24},{64... | collective-permute-start | bytes 1572872 | tf_op jit(solution)/shard_map/ppermute | solution.py:68
  79.9 20.9 %collective-permute-start.10 = (bf16[4,512,128]{2,1,0:T(8,128)(2,1)S(1)}, bf16[4,512,128]{2,1,0:T(8,128)(2,1)}, u32[]{:S(2)}, u32[]{:S(2)}) collective-permute-start(bf16[4,512,128]{2,1,0:T(8,128)(2,1)S(1)} %pad_maximum_fusion.6.kv0), channel_id=1, source_target_pairs={{0,64},{8,72},{16,80},{24,88},{32,96},{40,104},{48,112},{56,120},{... | collective-permute-start | bytes 1572872 | tf_op jit(solution)/shard_map/ppermute | solution.py:68
  80.0 34.6 %collective-permute-start.11 = (bf16[4,512,128]{2,1,0:T(8,128)(2,1)S(1)}, bf16[4,512,128]{2,1,0:T(8,128)(2,1)}, u32[]{:S(2)}, u32[]{:S(2)}) collective-permute-start(bf16[4,512,128]{2,1,0:T(8,128)(2,1)S(1)} %pad_maximum_fusion.6.kv0), channel_id=1, source_target_pairs={{0,32},{8,40},{16,48},{24,56},{32,64},{40,72},{48,80},{56,88},{64,... | collective-permute-start | bytes 1572872 | tf_op jit(solution)/shard_map/ppermute | solution.py:68
  278.6 219.6 %reduce-scatter.8.cloned.1.call-start = ((), (), s32[]{:S(2)}) async-start(), calls=%async_computation.8 | async-start | bytes 4456448 | tf_op jit(solution)/shard_map/reduce_scatter | solution.py:605
  284.9 249.6 %reduce-scatter.6.cloned.1.call-start = ((), (), s32[]{:S(2)}) async-start(), calls=%async_computation.7 | async-start | bytes 8912896 | tf_op jit(solution)/shard_map/reduce_scatter | solution.py:608
  309.9 92.4 %collective-permute-start.20 = (bf16[256,2048]{1,0:T(8,128)(2,1)}, bf16[256,2048]{1,0:T(8,128)(2,1)S(1)}, u32[]{:S(2)}, u32[]{:S(2)}) collective-permute-start(bf16[256,2048]{1,0:T(8,128)(2,1)} %slice.370), channel_id=1, source_target_pairs={{0,1},{1,0},{2,3},{3,2},{4,5},{5,4},{6,7},{7,6},{8,9},{9,8},{10,11... | collective-permute-start | bytes 3145736 | tf_op jit(solution)/shard_map/ppermute | solution.py:76
  319.5 65.6 %collective-permute-start.38 = (bf16[4,512,128]{2,1,0:T(8,128)(2,1)S(1)}, bf16[4,512,128]{2,1,0:T(8,128)(2,1)S(1)}, u32[]{:S(2)}, u32[]{:S(2)}) collective-permute-start(bf16[4,512,128]{2,1,0:T(8,128)(2,1)S(1)} %get-tuple-element.160), channel_id=1, source_target_pairs={{0,96},{8,104},{16,112},{24,120},{32,0},{40,8},{48,16},{56,24},{64... | collective-permute-start | bytes 1572872 | tf_op jit(solution)/shard_map/ppermute | solution.py:68
  357.6 27.5 %collective-permute-start.37 = (bf16[4,512,128]{2,1,0:T(8,128)(2,1)S(1)}, bf16[4,512,128]{2,1,0:T(8,128)(2,1)S(1)}, u32[]{:S(2)}, u32[]{:S(2)}) collective-permute-start(bf16[4,512,128]{2,1,0:T(8,128)(2,1)S(1)} %get-tuple-element.161), channel_id=1, source_target_pairs={{0,32},{8,40},{16,48},{24,56},{32,64},{40,72},{48,80},{56,88},{64,... | collective-permute-start | bytes 1572872 | tf_op jit(solution)/shard_map/ppermute | solution.py:68
  357.6 30.3 %collective-permute-start.36 = (bf16[4,512,128]{2,1,0:T(8,128)(2,1)S(1)}, bf16[4,512,128]{2,1,0:T(8,128)(2,1)S(1)}, u32[]{:S(2)}, u32[]{:S(2)}) collective-permute-start(bf16[4,512,128]{2,1,0:T(8,128)(2,1)S(1)} %get-tuple-element.159), channel_id=1, source_target_pairs={{0,64},{8,72},{16,80},{24,88},{32,96},{40,104},{48,112},{56,120},{... | collective-permute-start | bytes 1572872 | tf_op jit(solution)/shard_map/ppermute | solution.py:68
  416.5 33.9 %collective-permute-start.23 = (bf16[64,2048]{1,0:T(8,128)(2,1)S(1)}, bf16[64,2048]{1,0:T(8,128)(2,1)S(1)}, u32[]{:S(2)}, u32[]{:S(2)}) collective-permute-start(bf16[64,2048]{1,0:T(8,128)(2,1)S(1)} %get-tuple-element.174), channel_id=1, source_target_pairs={{0,6},{1,7},{2,0},{3,1},{4,2},{5,3},{6,4},{7,5},{8,14},{9,15},{10,... | collective-permute-start | bytes 786440 | tf_op jit(solution)/shard_map/ppermute | solution.py:72
  417.2 37.6 %collective-permute-start.22 = (bf16[64,2048]{1,0:T(8,128)(2,1)S(1)}, bf16[64,2048]{1,0:T(8,128)(2,1)S(1)}, u32[]{:S(2)}, u32[]{:S(2)}) collective-permute-start(bf16[64,2048]{1,0:T(8,128)(2,1)S(1)} %get-tuple-element.175), channel_id=1, source_target_pairs={{0,2},{1,3},{2,4},{3,5},{4,6},{5,7},{6,0},{7,1},{8,10},{9,11},{10,... | collective-permute-start | bytes 786440 | tf_op jit(solution)/shard_map/ppermute | solution.py:72
  421.0 20.6 %collective-permute-start.50 = (bf16[4,128,384]{2,1,0:T(8,128)(2,1)S(1)}, bf16[4,128,384]{2,1,0:T(8,128)(2,1)S(1)}, u32[]{:S(2)}, u32[]{:S(2)}) collective-permute-start(bf16[4,128,384]{2,1,0:T(8,128)(2,1)S(1)} %bitcast.201), channel_id=1, source_target_pairs={{0,64},{8,72},{16,80},{24,88},{32,96},{40,104},{48,112},{56,120},{... | collective-permute-start | bytes 1179656 | tf_op jit(solution)/shard_map/ppermute | solution.py:68
  445.5 17.4 %collective-permute-start.55 = (bf16[128,384]{1,0:T(8,128)(2,1)}, bf16[128,384]{1,0:T(8,128)(2,1)}, u32[]{:S(2)}, u32[]{:S(2)}) collective-permute-start(bf16[128,384]{1,0:T(8,128)(2,1)} %get-tuple-element.193), channel_id=1, source_target_pairs={{0,24},{8,0},{16,8},{24,16},{32,56},{40,32},{48,40},{56,48},{64,88... | collective-permute-start | bytes 294920 | tf_op jit(solution)/shard_map/ppermute | solution.py:64
  466.4 19.2 %collective-permute-start.46 = (bf16[64,2048]{1,0:T(8,128)(2,1)S(1)}, bf16[64,2048]{1,0:T(8,128)(2,1)S(1)}, u32[]{:S(2)}, u32[]{:S(2)}) collective-permute-start(bf16[64,2048]{1,0:T(8,128)(2,1)S(1)} %get-tuple-element.137), channel_id=1, source_target_pairs={{0,6},{1,7},{2,0},{3,1},{4,2},{5,3},{6,4},{7,5},{8,14},{9,15},{10,... | collective-permute-start | bytes 786440 | tf_op jit(solution)/shard_map/ppermute | solution.py:72
  468.3 17.3 %collective-permute-start.47 = (bf16[64,2048]{1,0:T(8,128)(2,1)S(1)}, bf16[64,2048]{1,0:T(8,128)(2,1)S(1)}, u32[]{:S(2)}, u32[]{:S(2)}) collective-permute-start(bf16[64,2048]{1,0:T(8,128)(2,1)S(1)} %get-tuple-element.137), channel_id=1, source_target_pairs={{0,4},{1,5},{2,6},{3,7},{4,0},{5,1},{6,2},{7,3},{8,12},{9,13},{10,... | collective-permute-start | bytes 786440 | tf_op jit(solution)/shard_map/ppermute | solution.py:72
  469.1 16.5 %collective-permute-start.48 = (bf16[64,2048]{1,0:T(8,128)(2,1)S(1)}, bf16[64,2048]{1,0:T(8,128)(2,1)}, u32[]{:S(2)}, u32[]{:S(2)}) collective-permute-start(bf16[64,2048]{1,0:T(8,128)(2,1)S(1)} %get-tuple-element.137), channel_id=1, source_target_pairs={{0,2},{1,3},{2,4},{3,5},{4,6},{5,7},{6,0},{7,1},{8,10},{9,11},{10,... | collective-permute-start | bytes 786440 | tf_op jit(solution)/shard_map/ppermute | solution.py:72
  474.7 21.4 %collective-permute-start.27 = (bf16[256,2048]{1,0:T(8,128)(2,1)S(1)}, bf16[256,2048]{1,0:T(8,128)(2,1)S(1)}, u32[]{:S(2)}, u32[]{:S(2)}) collective-permute-start(bf16[256,2048]{1,0:T(8,128)(2,1)S(1)} %pad_maximum_fusion.3), channel_id=1, source_target_pairs={{0,1},{1,0},{2,3},{3,2},{4,5},{5,4},{6,7},{7,6},{8,9},{9,8},{10,11... | collective-permute-start | bytes 3145736 | tf_op jit(solution)/shard_map/ppermute | solution.py:76
  487.6 67.4 %collective-permute-start.49 = (bf16[256,2048]{1,0:T(8,128)(2,1)}, bf16[256,2048]{1,0:T(8,128)(2,1)}, u32[]{:S(2)}, u32[]{:S(2)}) collective-permute-start(bf16[256,2048]{1,0:T(8,128)(2,1)} %pad_maximum_fusion.5), channel_id=1, source_target_pairs={{0,1},{1,0},{2,3},{3,2},{4,5},{5,4},{6,7},{7,6},{8,9},{9,8},{10,11... | collective-permute-start | bytes 3145736 | tf_op jit(solution)/shard_map/ppermute | solution.py:76
  (98 other events, 831.5 us)
Sparse Core Ops, SparseCore 0:
  10.7 56.3 all-gather.3
  69.8 92.0 all-gather.5
  164.6 56.3 all-gather.7
  278.7 67.8 reduce-scatter.3
  350.2 97.4 reduce-scatter.7
  451.0 83.4 reduce-scatter.5
